TPU v7x, 128 devices: a whole 4x4x4 slice. The times are simulated.
128 devices in a mesh: head: 4 (over x_lo, core), expert: 32 (over z, y, x_hi).
Axes of the slice: x: 4 (x_hi: 2, x_lo: 2; x = x_hi * 2 + x_lo), y: 4, z: 4, core: 2. Of those that a mesh axis runs over, the one named last changes fastest.
Arguments:
- attn: bfloat16 [4096, 4096], P('expert', 'head'), may hold values from -6 to 6
- o_weight: bfloat16 [4096, 4096], P('head'), may hold values from -0.09375 to 0.09375
- residual: bfloat16 [4096, 4096], P('expert'), may hold values from -6 to 6
- expert_ids: int32 [4096, 8], P('expert'), may hold values from 0 to 31, all different within a row; in each aligned block of 128 rows (0 to 127, 128 to 255, ...) at most 64 rows name the same one
- route_weight: bfloat16 [4096, 8], P('expert'), may hold values from 0.099609375 to 1
- gate_weight: bfloat16 [32, 4096, 1536], P('expert', None, 'head'), may hold values from -0.09375 to 0.09375
- up_weight: bfloat16 [32, 4096, 1536], P('expert', None, 'head'), may hold values from -0.09375 to 0.09375
Outputs:
- gram: float32 [32, 1536, 1536], P('expert', 'head')
Inputs may be any that keep to these rules, and one draw needn't show every extreme that they name: `expert_ids`: among the 128 rows of one device no expert is named more than 64 times, a bound that some block reaches; each row names 8 different experts.
All inputs are finite; a program needn't handle non-finite values.
Results may differ from a plain program's by a relative error of at most 0.0065.
Values may be sent and summed in bfloat16 or wider, within the bound.
No kernel may reach another device: no remote copies, remote signals or barrier semaphores. Data moves between devices by JAX's collectives and lax.ppermute only.
A program may use at most 128 MiB of HBM per device.

v0:
```python
import jax
import jax.numpy as jnp
from jax import lax
from jax.sharding import PartitionSpec as P


def body(attn, o_weight, residual, expert_ids, route_weight, gate_weight, up_weight):
    partial_value = jnp.dot(attn, o_weight, preferred_element_type=jnp.float32)
    width = residual.shape[1]
    mixed = residual.astype(jnp.float32) + lax.psum(partial_value, "head")
    squares = jnp.sum(mixed * mixed, axis=1)
    normed = (mixed * lax.rsqrt(squares / width + 1e-06)[:, None]).astype(jnp.bfloat16)
    owners = lax.axis_size("expert")
    tok_rows = expert_ids.shape[0]
    picks = expert_ids.shape[1]
    capacity = min(tok_rows, 2 * tok_rows * picks // owners)
    flat_ids = expert_ids.reshape(-1)
    hits = (flat_ids[:, None] == jnp.arange(owners, dtype=jnp.int32)[None, :]).astype(jnp.int32)
    before = jnp.cumsum(hits, axis=0) - hits
    rank = jnp.sum(before * hits, axis=1)
    slot_of = flat_ids * capacity + rank
    select = jnp.arange(owners * capacity, dtype=jnp.int32)[:, None] == slot_of[None, :]
    pick_rows = jnp.sum(
        select.reshape(owners * capacity, tok_rows, picks).astype(jnp.float32), axis=2
    ).astype(jnp.bfloat16)
    outgoing = jnp.dot(pick_rows, normed, preferred_element_type=jnp.float32).astype(jnp.bfloat16)
    out_weight = jnp.dot(
        select.astype(jnp.bfloat16), route_weight.reshape(-1), preferred_element_type=jnp.float32
    ).astype(jnp.bfloat16)
    outgoing = outgoing.reshape(owners, capacity, outgoing.shape[1])
    out_weight = out_weight.reshape(owners, capacity)
    received, got_weight = (
        lax.all_to_all(outgoing, "expert", split_axis=0, concat_axis=0, tiled=True),
        lax.all_to_all(out_weight, "expert", split_axis=0, concat_axis=0, tiled=True),
    )
    received = received.reshape(owners * capacity, received.shape[2])
    weights = got_weight.reshape(-1).astype(jnp.float32)
    w_gate = gate_weight[0]
    w_up = up_weight[0]
    gate = jnp.dot(received, w_gate, preferred_element_type=jnp.float32)
    up = jnp.dot(received, w_up, preferred_element_type=jnp.float32)
    keys = (jax.nn.silu(gate) * up).astype(jnp.bfloat16)
    scaled = (keys.astype(jnp.float32) * weights[:, None]).astype(jnp.bfloat16)
    total = jnp.sum(weights)
    block = lax.dot_general(
        scaled,
        lax.all_gather(keys, "head", axis=1, tiled=True),
        (((0,), (0,)), ((), ())),
        preferred_element_type=jnp.float32,
    )
    return (block / total)[None]


def solution(mesh):
    return jax.shard_map(
        body,
        mesh=mesh,
        in_specs=(
            P("expert", "head"),
            P("head", None),
            P("expert", None),
            P("expert", None),
            P("expert", None),
            P("expert", None, "head"),
            P("expert", None, "head"),
        ),
        out_specs=P("expert", "head", None),
        check_vma=False,
    )
```

profile of v0, /device:TPU:1, one launch (start us, length us, event | category | flops | bytes accessed | tf_op | source)
XLA Modules:
  0.0 379.8 jit_solution(18009387903659166094)
XLA Ops:
  6.5 0.0 copy-start
  6.5 0.0 copy-start.2
  6.5 0.0 all-reduce.2.cloned.1.call-start
  6.5 6.2 %fusion.16 = f32[128,4096]{1,0:T(8,128)} fusion(bf16[128,1024]{1,0:T(8,128)(2,1)} %param.7, bf16[1024,4096]{1,0:T(8,128)(2,1)} %param.8), kind=kOutput, calls=%fused_computation.33 | convolution fusion | flops 1073741824 | bytes 10747904 | tf_op jit(solution)/shard_map/dot_general | solution.py:8
  12.7 0.0 all-reduce.2.cloned.1.call-update
  12.8 0.0 all-gather.2.cloned.1.call-start
  12.8 0.0 copy-done.2
  12.8 0.1 copy.33
  12.9 0.1 eq.50
  13.0 0.1 eq.46
  13.1 9.0 %reduce-window.6 = s32[32,8,128]{2,1,0:T(8,128)S(1)} reduce-window(s32[32,8,128]{2,1,0:T(8,128)S(1)} %fusion.15, s32[]{:T(128)} %constant.7.clone.1), window={size=1x1x128 pad=0_0x0_0x127_0}, to_apply=%region_0.0 | reduce-window | flops 4161536 | bytes 262148 | tf_op jit(solution)/shard_map/reduce-window
  22.2 0.1 slice.8
  22.3 0.1 copy.35
  22.4 0.1 copy.36
  22.5 0.1 broadcast_add_fusion
  22.7 0.1 reduce_sum.39
  22.8 11.5 %convert_reduce_fusion = bf16[2048,128]{1,0:T(8,128)(2,1)} fusion(s32[128,8]{0,1:T(8,128)S(1)} %multiply_add_fusion.1), kind=kLoop, calls=%fused_computation.2 | loop fusion | flops 6029312 | bytes 528384 | tf_op jit(solution)/shard_map/reduce_sum | solution.py:23
  34.3 39.5 %all-reduce.2.cloned.1.call-done = f32[128,4096]{1,0:T(8,128)} async-done(((f32[128,4096]{1,0:T(8,128)}), f32[128,4096]{1,0:T(8,128)}) %all-reduce.2.cloned.1.call-update) | async-done | bytes 2097168 | tf_op jit(solution)/shard_map/psum | solution.py:10
  73.8 2.2 multiply_reduce_fusion
  76.0 12.3 %convolution_convert_fusion = bf16[2048,4096]{1,0:T(8,128)(2,1)} fusion(f32[128,4096]{1,0:T(8,128)} %all-reduce.2.cloned.1.call-done, bf16[128,4096]{1,0:T(8,128)(2,1)} %param.9, f32[128]{0:T(128)S(1)} %add_rsqrt_fusion, bf16[2048,128]{1,0:T(8,128)(2,1)} %convert_reduce_fusion), kind=kOutput, calls=%fused_computation | convolution fusion | flops 2157969408 | bytes 20447744 | tf_op jit(solution)/shard_map/dot_general | solution.py:26
  88.4 196.1 %all_to_all.15 = bf16[32,64,4096]{2,1,0:T(8,128)(2,1)S(1)} all-to-all(bf16[32,64,4096]{2,1,0:T(8,128)(2,1)} %bitcast.38), channel_id=1, replica_groups=mesh['head'=4,'expert'=32] {'expert'}, dimensions={0} | all-to-all | bytes 33554432 | tf_op jit(solution)/shard_map/all_to_all | solution.py:33
  284.5 0.0 copy-done
  284.5 0.0 copy-start.4
  284.5 8.9 %fusion.3 = f32[2048,384]{1,0:T(8,128)S(1)} fusion(bf16[2048,4096]{1,0:T(8,128)(2,1)S(1)} %bitcast.39, bf16[1,4096,384]{2,1,0:T(8,128)(2,1)S(1)} %copy-done), kind=kOutput, calls=%fused_computation.8 | convolution fusion | flops 6442450944 | bytes 23068672 | tf_op jit(solution)/shard_map/dot_general | solution.py:40
  293.4 0.0 copy-done.4
  293.4 0.0 copy-start.3
  293.4 10.0 %fusion.6 = bf16[2048,384]{1,0:T(8,128)(2,1)} fusion(bf16[2048,4096]{1,0:T(8,128)(2,1)S(1)} %bitcast.40, bf16[1,4096,384]{2,1,0:T(8,128)(2,1)S(1)} %copy-done.4, f32[2048,384]{1,0:T(8,128)S(1)} %fusion.3), kind=kOutput, calls=%fused_computation.13 | convolution fusion | flops 6447169536 | bytes 24641536 | tf_op jit(solution)/shard_map/dot_general | solution.py:41
  303.4 0.0 all-gather.2.cloned.1.call-update
  303.5 0.0 copy-done.3
  303.5 0.1 copy.38
  303.6 0.1 reshape.69
  303.7 1.5 fusion
  305.2 0.1 all_to_all.12
  305.3 12.0 %all_to_all.16 = bf16[32,1,64]{2,1,0:T(2,128)(2,1)S(1)} all-to-all(bf16[32,1,64]{2,1,0:T(2,128)(2,1)S(1)} %all_to_all.12), channel_id=1, replica_groups=mesh['head'=4,'expert'=32] {'expert'}, dimensions={0} | all-to-all | bytes 8192 | tf_op jit(solution)/shard_map/all_to_all | solution.py:34
  317.3 0.7 convert_reduce_fusion.1
  318.0 0.1 reshape.68
  318.1 46.6 %all-gather.2.cloned.1.call-done = bf16[2048,1536]{1,0:T(8,128)(2,1)} async-done(((bf16[2048,384]{1,0:T(8,128)(2,1)}), bf16[2048,1536]{1,0:T(8,128)(2,1)}) %all-gather.2.cloned.1.call-update) | async-done | bytes 6291472 | tf_op jit(solution)/shard_map/all_gather | solution.py:47
  364.7 0.0 copy-start.1
  364.7 8.3 %fusion.5 = f32[1,384,1536]{2,1,0:T(8,128)} fusion(bf16[2048,1536]{1,0:T(8,128)(2,1)} %all-gather.2.cloned.1.call-done, bf16[2048,384]{1,0:T(8,128)(2,1)} %fusion.6, f32[2048]{0:T(1024)S(1)} %reshape.68, f32[]{:T(128)} %get-tuple-element.5), kind=kOutput, calls=%fused_computation.12 | convolution fusion | flops 2418868224 | bytes 10231812 | tf_op jit(solution)/shard_map/dot_general | solution.py:45
  373.0 0.0 copy-done.1
  (9 shorter events, 0.2 us)
Async XLA Ops:
  6.5 278.0 %copy-start = (bf16[1,4096,384]{2,1,0:T(8,128)(2,1)S(1)}, bf16[1,4096,384]{2,1,0:T(8,128)(2,1)}, u32[]{:S(2)}) copy-start(bf16[1,4096,384]{2,1,0:T(8,128)(2,1)} %param.12) | copy-start | bytes 9437188
  6.5 6.3 %copy-start.2 = (s32[128,8]{0,1:T(8,128)S(1)}, s32[128,8]{0,1:T(8,128)}, u32[]{:S(2)}) copy-start(s32[128,8]{0,1:T(8,128)} %param.10) | copy-start | bytes 12292
  6.5 67.3 %all-reduce.2.cloned.1.call-start = ((), (), s32[]{:S(2)}) async-start(), calls=%async_computation.2 | async-start | bytes 4194304 | tf_op jit(solution)/shard_map/psum | solution.py:10
  12.8 351.9 %all-gather.2.cloned.1.call-start = ((), (), s32[]{:S(2)}) async-start(), calls=%async_computation.3 | async-start | bytes 7864320 | tf_op jit(solution)/shard_map/all_gather | solution.py:47
  284.5 8.9 %copy-start.4 = (bf16[1,4096,384]{2,1,0:T(8,128)(2,1)S(1)}, bf16[1,4096,384]{2,1,0:T(8,128)(2,1)}, u32[]{:S(2)}) copy-start(bf16[1,4096,384]{2,1,0:T(8,128)(2,1)} %param.13) | copy-start | bytes 9437188
  293.4 10.1 %copy-start.3 = (bf16[128,8]{0,1:T(8,128)(2,1)S(1)}, bf16[128,8]{0,1:T(8,128)(2,1)}, u32[]{:S(2)}) copy-start(bf16[128,8]{0,1:T(8,128)(2,1)} %param.11) | copy-start | bytes 6148
  364.7 8.3 %copy-start.1 = (bf16[1,4096,384]{2,1,0:T(8,128)(2,1)S(1)}, bf16[1,4096,384]{2,1,0:T(8,128)(2,1)}, u32[]{:S(2)}) copy-start(bf16[1,4096,384]{2,1,0:T(8,128)(2,1)} %param.12) | copy-start | bytes 9437188
Sparse Core Ops, SparseCore 0:
  12.9 60.8 all-reduce.1
  303.6 61.0 all-gather.1
where the time goes:
time: 380 us
  blocking collectives  208 us (55%)
  waiting for transfers between devices  86.1 us (23%)
  matrix products  47.2 us (12%)
  other arithmetic  23.7 us (6%)
  between operations  13.5 us (4%)
    all_to_all x1, blocking collectives, body(): lax.all_to_all(outgoing, 'expert', split_axis=0, concat_axis=0, tiled=True)  196 us
    all_gather x1, waiting for transfers between devices, body(): lax.all_gather(keys, 'head', axis=1, tiled=True)  46.6 us
    psum x1, waiting for transfers between devices, body(): mixed = residual.astype(jnp.float32) + lax.psum(partial_value, 'head')  39.5 us
    dot_general x1, matrix products, body(): jnp.dot(pick_rows, normed, preferred_element_type=jnp.float32)  12.3 us
    all_to_all x1, blocking collectives, body(): lax.all_to_all(out_weight, 'expert', split_axis=0, concat_axis=0, tiled=T...  12 us
    reduce_sum x1, other arithmetic, body(): jnp.sum(select.reshape(owners * capacity, tok_rows, picks).astype(jnp.flo...  11.5 us
    dot_general x1, matrix products, body(): up = jnp.dot(received, w_up, preferred_element_type=jnp.float32)  10 us
    another operation x3, other arithmetic  9.15 us
  transfers between devices with their start and end apart: 2, of which 2 were waited for; matrix products, arithmetic and copies ran while one was open for 6% of the time, Pallas kernels for 0%

commit v1 on v0

--- a/solution.py
+++ b/solution.py
@@ -7,7 +7,7 @@
 def body(attn, o_weight, residual, expert_ids, route_weight, gate_weight, up_weight):
     partial_value = jnp.dot(attn, o_weight, preferred_element_type=jnp.float32)
     width = residual.shape[1]
-    mixed = residual.astype(jnp.float32) + lax.psum(partial_value, "head")
+    mixed = residual.astype(jnp.float32) + jnp.sum(lax.all_gather(partial_value, "head"), axis=0)
     squares = jnp.sum(mixed * mixed, axis=1)
     normed = (mixed * lax.rsqrt(squares / width + 1e-06)[:, None]).astype(jnp.bfloat16)
     owners = lax.axis_size("expert")

time: 380 us -> 434 us (1.14)
  waiting for transfers between devices: 86.1 us -> 119 us
  blocking collectives: 208 us -> 224 us
  other arithmetic: 23.7 us -> 29.2 us
    all_gather x0 -> x1, waiting for transfers between devices: none -> 63.6 us  [body(): lax.all_gather(partial_value, 'head')]
    psum x1 -> x0, waiting for transfers between devices: 39.5 us -> none  [body(): mixed = residual.astype(jnp.float32) + lax.psum(partial_value, 'head')]
    all_to_all x1, blocking collectives: 12 us -> 22.4 us  [body(): lax.all_to_all(out_weight, 'expert', split_axis=0, concat_axis=0, tiled=T...]
    all_gather x1, waiting for transfers between devices: 46.6 us -> 55.6 us  [body(): lax.all_gather(keys, 'head', axis=1, tiled=True)]
    reduce_sum x0 -> x1, other arithmetic: none -> 5.5 us  [body(): jnp.sum(lax.all_gather(partial_value, 'head'), axis=0)]
    all_to_all x1, blocking collectives: 196 us -> 201 us  [body(): lax.all_to_all(outgoing, 'expert', split_axis=0, concat_axis=0, tiled=True)]
where the time goes in v1:
time: 434 us
  blocking collectives  224 us (52%)
  waiting for transfers between devices  119 us (27%)
  matrix products  47.2 us (11%)
  other arithmetic  29.2 us (7%)
  between operations  13.5 us (3%)
    all_to_all x1, blocking collectives, body(): lax.all_to_all(outgoing, 'expert', split_axis=0, concat_axis=0, tiled=True)  201 us
    all_gather x1, waiting for transfers between devices, body(): lax.all_gather(partial_value, 'head')  63.6 us
    all_gather x1, waiting for transfers between devices, body(): lax.all_gather(keys, 'head', axis=1, tiled=True)  55.6 us
    all_to_all x1, blocking collectives, body(): lax.all_to_all(out_weight, 'expert', split_axis=0, concat_axis=0, tiled=T...  22.4 us
    dot_general x1, matrix products, body(): jnp.dot(pick_rows, normed, preferred_element_type=jnp.float32)  12.3 us
    reduce_sum x1, other arithmetic, body(): jnp.sum(select.reshape(owners * capacity, tok_rows, picks).astype(jnp.flo...  11.5 us
    dot_general x1, matrix products, body(): up = jnp.dot(received, w_up, preferred_element_type=jnp.float32)  10 us
    another operation x3, other arithmetic  9.15 us
  transfers between devices with their start and end apart: 2, of which 2 were waited for; matrix products, arithmetic and copies ran while one was open for 6% of the time, Pallas kernels for 0%

profile of v1, /device:TPU:1, one launch (start us, length us, event | category | flops | bytes accessed | tf_op | source)
XLA Modules:
  0.0 434.2 jit_solution(4427790999641756466)
XLA Ops:
  6.5 0.0 copy-start
  6.5 0.0 copy-start.2
  6.5 0.0 all-gather.6.cloned.1.call-start
  6.5 6.2 %fusion.16 = f32[128,4096]{1,0:T(8,128)} fusion(bf16[128,1024]{1,0:T(8,128)(2,1)} %param.7, bf16[1024,4096]{1,0:T(8,128)(2,1)} %param.8), kind=kOutput, calls=%fused_computation.33 | convolution fusion | flops 1073741824 | bytes 10747904 | tf_op jit(solution)/shard_map/dot_general | solution.py:8
  12.7 0.0 all-gather.6.cloned.1.call-update
  12.8 0.0 all-gather.4.cloned.1.call-start
  12.8 0.0 copy-done.2
  12.8 0.1 copy.33
  12.9 0.1 eq.50
  13.0 0.1 eq.46
  13.1 9.0 %reduce-window.6 = s32[32,8,128]{2,1,0:T(8,128)S(1)} reduce-window(s32[32,8,128]{2,1,0:T(8,128)S(1)} %fusion.15, s32[]{:T(128)} %constant.7.clone.1), window={size=1x1x128 pad=0_0x0_0x127_0}, to_apply=%region_0.0 | reduce-window | flops 4161536 | bytes 262148 | tf_op jit(solution)/shard_map/reduce-window
  22.2 0.1 slice.8
  22.3 0.1 copy.35
  22.4 0.1 copy.36
  22.5 0.1 broadcast_add_fusion
  22.7 0.1 reduce_sum.48
  22.8 11.5 %convert_reduce_fusion = bf16[2048,128]{1,0:T(8,128)(2,1)} fusion(s32[128,8]{0,1:T(8,128)S(1)} %multiply_add_fusion.1), kind=kLoop, calls=%fused_computation.2 | loop fusion | flops 6029312 | bytes 528384 | tf_op jit(solution)/shard_map/reduce_sum | solution.py:23
  34.3 63.6 %all-gather.6.cloned.1.call-done = f32[512,4096]{1,0:T(8,128)} async-done(((f32[128,4096]{1,0:T(8,128)}), f32[512,4096]{1,0:T(8,128)}) %all-gather.6.cloned.1.call-update) | async-done | bytes 8388624 | tf_op jit(solution)/shard_map/all_gather | solution.py:10
  97.9 5.5 %reduce_sum.50 = f32[128,4096]{1,0:T(8,128)} reduce(f32[4,128,4096]{2,1,0:T(8,128)} %bitcast.42, f32[]{:T(128)} %constant.14.clone.1), dimensions={0}, to_apply=%region_4.5 | reduce | flops 1572864 | bytes 10485764 | tf_op jit(solution)/shard_map/reduce_sum | solution.py:10
  103.5 2.2 multiply_reduce_fusion
  105.7 12.3 %convolution_convert_fusion = bf16[2048,4096]{1,0:T(8,128)(2,1)} fusion(f32[128,4096]{1,0:T(8,128)} %reduce_sum.50, bf16[128,4096]{1,0:T(8,128)(2,1)} %param.9, f32[128]{0:T(128)S(1)} %add_rsqrt_fusion, bf16[2048,128]{1,0:T(8,128)(2,1)} %convert_reduce_fusion), kind=kOutput, calls=%fused_computation | convolution fusion | flops 2157969408 | bytes 20447744 | tf_op jit(solution)/shard_map/dot_general | solution.py:26
  118.0 201.5 %all_to_all.15 = bf16[32,64,4096]{2,1,0:T(8,128)(2,1)S(1)} all-to-all(bf16[32,64,4096]{2,1,0:T(8,128)(2,1)} %bitcast.39), channel_id=1, replica_groups=mesh['head'=4,'expert'=32] {'expert'}, dimensions={0} | all-to-all | bytes 33554432 | tf_op jit(solution)/shard_map/all_to_all | solution.py:33
  319.5 0.0 copy-done
  319.5 0.0 copy-start.4
  319.5 8.9 %fusion.3 = f32[2048,384]{1,0:T(8,128)S(1)} fusion(bf16[2048,4096]{1,0:T(8,128)(2,1)S(1)} %bitcast.40, bf16[1,4096,384]{2,1,0:T(8,128)(2,1)S(1)} %copy-done), kind=kOutput, calls=%fused_computation.8 | convolution fusion | flops 6442450944 | bytes 23068672 | tf_op jit(solution)/shard_map/dot_general | solution.py:40
  328.4 0.0 copy-done.4
  328.4 0.0 copy-start.3
  328.4 10.0 %fusion.6 = bf16[2048,384]{1,0:T(8,128)(2,1)} fusion(bf16[2048,4096]{1,0:T(8,128)(2,1)S(1)} %bitcast.41, bf16[1,4096,384]{2,1,0:T(8,128)(2,1)S(1)} %copy-done.4, f32[2048,384]{1,0:T(8,128)S(1)} %fusion.3), kind=kOutput, calls=%fused_computation.13 | convolution fusion | flops 6447169536 | bytes 24641536 | tf_op jit(solution)/shard_map/dot_general | solution.py:41
  338.4 0.0 all-gather.4.cloned.1.call-update
  338.5 0.0 copy-done.3
  338.5 0.1 copy.38
  338.6 0.1 reshape.70
  338.7 1.5 fusion
  340.2 0.1 all_to_all.12
  340.3 22.4 %all_to_all.16 = bf16[32,1,64]{2,1,0:T(2,128)(2,1)S(1)} all-to-all(bf16[32,1,64]{2,1,0:T(2,128)(2,1)S(1)} %all_to_all.12), channel_id=1, replica_groups=mesh['head'=4,'expert'=32] {'expert'}, dimensions={0} | all-to-all | bytes 8192 | tf_op jit(solution)/shard_map/all_to_all | solution.py:34
  362.7 0.7 convert_reduce_fusion.1
  363.4 0.1 reshape.68
  363.5 55.6 %all-gather.4.cloned.1.call-done = bf16[2048,1536]{1,0:T(8,128)(2,1)} async-done(((bf16[2048,384]{1,0:T(8,128)(2,1)}), bf16[2048,1536]{1,0:T(8,128)(2,1)}) %all-gather.4.cloned.1.call-update) | async-done | bytes 6291472 | tf_op jit(solution)/shard_map/all_gather | solution.py:47
  419.1 0.0 copy-start.1
  419.1 8.3 %fusion.5 = f32[1,384,1536]{2,1,0:T(8,128)} fusion(bf16[2048,1536]{1,0:T(8,128)(2,1)} %all-gather.4.cloned.1.call-done, bf16[2048,384]{1,0:T(8,128)(2,1)} %fusion.6, f32[2048]{0:T(1024)S(1)} %reshape.68, f32[]{:T(128)} %get-tuple-element.5), kind=kOutput, calls=%fused_computation.12 | convolution fusion | flops 2418868224 | bytes 10231812 | tf_op jit(solution)/shard_map/dot_general | solution.py:45
  427.4 0.0 copy-done.1
  (9 shorter events, 0.2 us)
Async XLA Ops:
  6.5 313.0 %copy-start = (bf16[1,4096,384]{2,1,0:T(8,128)(2,1)S(1)}, bf16[1,4096,384]{2,1,0:T(8,128)(2,1)}, u32[]{:S(2)}) copy-start(bf16[1,4096,384]{2,1,0:T(8,128)(2,1)} %param.12) | copy-start | bytes 9437188
  6.5 6.3 %copy-start.2 = (s32[128,8]{0,1:T(8,128)S(1)}, s32[128,8]{0,1:T(8,128)}, u32[]{:S(2)}) copy-start(s32[128,8]{0,1:T(8,128)} %param.10) | copy-start | bytes 12292
  6.5 91.4 %all-gather.6.cloned.1.call-start = ((), (), s32[]{:S(2)}) async-start(), calls=%async_computation.3 | async-start | bytes 10485760 | tf_op jit(solution)/shard_map/all_gather | solution.py:10
  12.8 406.3 %all-gather.4.cloned.1.call-start = ((), (), s32[]{:S(2)}) async-start(), calls=%async_computation.2 | async-start | bytes 7864320 | tf_op jit(solution)/shard_map/all_gather | solution.py:47
  319.5 8.9 %copy-start.4 = (bf16[1,4096,384]{2,1,0:T(8,128)(2,1)S(1)}, bf16[1,4096,384]{2,1,0:T(8,128)(2,1)}, u32[]{:S(2)}) copy-start(bf16[1,4096,384]{2,1,0:T(8,128)(2,1)} %param.13) | copy-start | bytes 9437188
  328.4 10.1 %copy-start.3 = (bf16[128,8]{0,1:T(8,128)(2,1)S(1)}, bf16[128,8]{0,1:T(8,128)(2,1)}, u32[]{:S(2)}) copy-start(bf16[128,8]{0,1:T(8,128)(2,1)} %param.11) | copy-start | bytes 6148
  419.1 8.3 %copy-start.1 = (bf16[1,4096,384]{2,1,0:T(8,128)(2,1)S(1)}, bf16[1,4096,384]{2,1,0:T(8,128)(2,1)}, u32[]{:S(2)}) copy-start(bf16[1,4096,384]{2,1,0:T(8,128)(2,1)} %param.12) | copy-start | bytes 9437188
Sparse Core Ops, SparseCore 0:
  12.9 85.0 all-gather.5
  338.6 80.4 all-gather.3
